TPU v7x, 32 devices: a whole 2x2x4 slice. The times are simulated.
32 devices in a mesh: groups: 2 (over y), tensor: 16 (over z, x, core).
Axes of the slice: x: 2, y: 2, z: 4, core: 2. Of those that a mesh axis runs over, the one named last changes fastest.
Arguments:
- inputs: bfloat16 [256, 8192], P(('groups', 'tensor')), parts along dimension 0, may hold values from -6 to 6
- tangent: bfloat16 [256, 8192], P(('groups', 'tensor')), parts along dimension 0, may hold values from -6 to 6
- token_ids: int32 [256], P('groups'), parts along dimension 0, may hold values from 0 to 64127
- gate_weight: bfloat16 [8192, 28672], P(None, 'tensor'), may hold values from -0.0625 to 0.0625
- up_weight: bfloat16 [8192, 28672], P(None, 'tensor'), may hold values from -0.0625 to 0.0625
- down_weight: bfloat16 [28672, 8192], P('tensor'), may hold values from -0.046875 to 0.046875
- sketch: bfloat16 [8192, 1024], P('tensor'), may hold values from -0.09375 to 0.09375
- teacher_precision: bfloat16 [64128, 1024], P(None, 'tensor'), may hold values from 0.099609375 to 10
Outputs:
- curvature: float32 [256, 8192], P(('groups', 'tensor')), parts along dimension 0
There are 2 independent parts, one for each index of `groups`. A program takes and returns all parts, laid end to end along the dimension named above; an argument that names none is the same for every part. Nothing has to cross between parts.
All inputs are finite; a program needn't handle non-finite values.
Results may differ from a plain program's by a relative error of at most 0.006.
Values may be sent and summed in bfloat16 or wider, within the bound.
A program may use at most 256 MiB of HBM per device.

v0:
```python
import jax
import jax.numpy as jnp
from jax import lax
from jax.sharding import PartitionSpec as P


def on_device(
    inputs, tangent, token_ids, gate_weight, up_weight, down_weight, sketch, teacher_precision
):
    rows_x, rows_v = (
        lax.all_gather(inputs, "tensor", axis=0, tiled=True),
        lax.all_gather(tangent, "tensor", axis=0, tiled=True),
    )
    position = lax.axis_index("tensor")
    feat_local = sketch.shape[0]
    offset = position * feat_local
    pre_gate = jnp.dot(rows_x, gate_weight, preferred_element_type=jnp.float32)
    pre_up = jnp.dot(rows_x, up_weight, preferred_element_type=jnp.float32)
    tan_gate = jnp.dot(rows_v, gate_weight, preferred_element_type=jnp.float32)
    tan_up = jnp.dot(rows_v, up_weight, preferred_element_type=jnp.float32)
    sig = jax.nn.sigmoid(pre_gate)
    act = pre_gate * sig
    slope = sig * (1.0 + pre_gate * (1.0 - sig))
    tan_hidden = (slope * tan_gate * pre_up + act * tan_up).astype(jnp.bfloat16)
    v_mine = lax.dynamic_slice_in_dim(rows_v, offset, feat_local, 1)
    own_term = jnp.dot(v_mine, sketch, preferred_element_type=jnp.float32)
    partial_value = jnp.dot(tan_hidden, down_weight, preferred_element_type=jnp.float32)
    summed_cols = lax.psum_scatter(partial_value, "tensor", scatter_dimension=1, tiled=True)
    sketch_part = (
        jnp.dot(summed_cols, sketch.astype(jnp.float32), precision=lax.Precision.HIGHEST) + own_term
    )
    sketch_cols = lax.psum_scatter(sketch_part, "tensor", scatter_dimension=1, tiled=True)
    rows_prec = teacher_precision[token_ids].astype(jnp.float32)
    weighted_cols = (rows_prec * sketch_cols).astype(jnp.bfloat16)
    weighted = lax.all_gather(weighted_cols, "tensor", axis=1, tiled=True)
    cot_cols = jnp.dot(weighted, sketch.T, preferred_element_type=jnp.float32)
    cot_full = lax.all_gather(cot_cols.astype(jnp.bfloat16), "tensor", axis=1, tiled=True)
    back_hidden = jnp.dot(cot_full, down_weight.T, preferred_element_type=jnp.float32)
    back_gate = (back_hidden * pre_up * slope).astype(jnp.bfloat16)
    back_up = (back_hidden * act).astype(jnp.bfloat16)
    result = jnp.dot(back_gate, gate_weight.T, preferred_element_type=jnp.float32)
    result = result + jnp.dot(back_up, up_weight.T, preferred_element_type=jnp.float32)
    current = lax.dynamic_slice_in_dim(result, offset, feat_local, 1)
    return lax.psum_scatter(
        lax.dynamic_update_slice_in_dim(result, current + cot_cols, offset, 1),
        "tensor",
        scatter_dimension=0,
        tiled=True,
    )


def solution(mesh):
    return jax.shard_map(
        on_device,
        mesh=mesh,
        in_specs=(
            P(("groups", "tensor"), None),
            P(("groups", "tensor"), None),
            P("groups"),
            P(None, "tensor"),
            P(None, "tensor"),
            P("tensor", None),
            P("tensor", None),
            P(None, "tensor"),
        ),
        out_specs=P(("groups", "tensor"), None),
        check_vma=False,
    )
```

profile of v0, /device:TPU:0, one launch (start us, length us, event | category | flops | bytes accessed | tf_op | source)
XLA Modules:
  0.0 454.1 jit_solution(6190567908116043096)
XLA Ops:
  6.5 0.0 copy-start
  6.5 0.0 all-gather.4.cloned.1.call-start
  6.5 0.7 all-gather.4.cloned.1.call-update
  7.3 0.0 all-gather.6.cloned.1.call-start
  7.3 0.7 all-gather.6.cloned.1.call-update
  8.0 0.0 reduce-scatter.6.cloned.1.call-start
  8.1 45.6 %all-gather.4.cloned.1.call-done = bf16[128,8192]{1,0:T(8,128)(2,1)} async-done(((bf16[8,8192]{1,0:T(8,128)(2,1)}), bf16[128,8192]{1,0:T(8,128)(2,1)}) %all-gather.4.cloned.1.call-update) | async-done | bytes 2097168 | tf_op jit(solution)/shard_map/all_gather | solution.py:11
  53.7 0.0 copy-start.3
  53.7 15.2 %fusion.13 = f32[128,1792]{1,0:T(8,128)} fusion(bf16[128,8192]{1,0:T(8,128)(2,1)} %all-gather.4.cloned.1.call-done, bf16[8192,1792]{1,0:T(8,128)(2,1)} %param.11), kind=kOutput, calls=%fused_computation.24 | convolution fusion | flops 3758096384 | bytes 32374784 | tf_op jit(solution)/shard_map/dot_general | solution.py:17
  68.8 0.0 copy-done.3
  68.8 12.4 %fusion.14 = f32[128,1792]{1,0:T(8,128)} fusion(bf16[128,8192]{1,0:T(8,128)(2,1)S(1)} %copy-done.3, bf16[8192,1792]{1,0:T(8,128)(2,1)} %param.12), kind=kOutput, calls=%fused_computation.25 | convolution fusion | flops 3758096384 | bytes 32374784 | tf_op jit(solution)/shard_map/dot_general | solution.py:18
  81.3 14.8 %all-gather.6.cloned.1.call-done = bf16[128,8192]{1,0:T(8,128)(2,1)} async-done(((bf16[8,8192]{1,0:T(8,128)(2,1)}), bf16[128,8192]{1,0:T(8,128)(2,1)}) %all-gather.6.cloned.1.call-update) | async-done | bytes 2097168 | tf_op jit(solution)/shard_map/all_gather | solution.py:12
  96.0 0.0 copy-start.1
  96.0 15.6 %fusion = f32[128,1792]{1,0:T(8,128)} fusion(f32[128,1792]{1,0:T(8,128)} %fusion.14, bf16[128,8192]{1,0:T(8,128)(2,1)} %all-gather.6.cloned.1.call-done, bf16[8192,1792]{1,0:T(8,128)(2,1)} %param.11, f32[128,1792]{1,0:T(8,128)} %fusion.13), kind=kOutput, calls=%fused_computation.4 | convolution fusion | flops 3760160768 | bytes 34209792 | tf_op jit(solution)/shard_map/dot_general | solution.py:19
  111.7 0.0 copy-done.1
  111.7 24.0 %fusion.3 = f32[128,8192]{1,0:T(8,128)} fusion(bf16[1792,8192]{1,0:T(8,128)(2,1)} %param.13, f32[128,1792]{1,0:T(8,128)} %fusion, bf16[128,8192]{1,0:T(8,128)(2,1)S(1)} %copy-done.1, bf16[8192,1792]{1,0:T(8,128)(2,1)} %param.12, f32[128,1792]{1,0:T(8,128)} %fusion.13), kind=kOutput, calls=%fused_computation.7 | convolution fusion | flops 7517798400 | bytes 66846720 | tf_op jit(solution)/shard_map/dot_general | solution.py:27
  135.7 0.0 reduce-scatter.6.cloned.1.call-update
  135.7 0.0 reduce-scatter.10.cloned.1.call-start
  135.8 71.2 %reduce-scatter.6.cloned.1.call-done = f32[128,512]{1,0:T(8,128)} async-done(((f32[128,8192]{1,0:T(8,128)}), f32[128,512]{1,0:T(8,128)}) %reduce-scatter.6.cloned.1.call-update) | async-done | bytes 262160 | tf_op jit(solution)/shard_map/reduce_scatter | solution.py:28
  206.9 0.0 copy-done
  206.9 1.5 fusion.15
  208.5 1.1 convolution_add_fusion.1
  209.6 2.0 copy.12
  211.6 0.0 reduce-scatter.10.cloned.1.call-update
  211.6 0.0 copy-start.4
  211.7 0.0 all-gather.8.cloned.1.call-start
  211.7 15.8 %copy.10 = bf16[64128,64]{1,0:T(8,128)(2,1)} copy(bf16[64128,64]{0,1:T(8,128)(2,1)} %param.15) | data formatting | bytes 16416768 | tf_op args[7]
  227.5 0.0 copy-done.4
  227.5 8.5 %gather_fusion = bf16[128,64]{1,0:T(8,128)(2,1)S(1)} fusion(bf16[64128,64]{1,0:T(8,128)(2,1)} %copy.10, s32[1024]{0:T(1024)S(1)} %pad_clamp_fusion), kind=kCustom, calls=%fused_computation | custom fusion | bytes 33280 | tf_op jit(solution)/shard_map/gather | solution.py:33
  236.0 30.7 %reduce-scatter.10.cloned.1.call-done = f32[64,128]{1,0:T(8,128)} async-done(((f32[1024,128]{1,0:T(8,128)}), f32[64,128]{1,0:T(8,128)}) %reduce-scatter.10.cloned.1.call-update) | async-done | bytes 32784
  266.7 0.8 copy.13
  267.6 0.1 copy.11
  267.6 20.1 %all_gather.14 = bf16[128,1024]{0,1:T(8,128)(2,1)S(1)} all-gather(bf16[128,64]{0,1:T(8,128)(2,1)S(1)} %copy.11), channel_id=1, replica_groups=mesh['groups'=2,'tensor'=16] {'tensor'}, dimensions={1}, use_global_device_ids=true | all-gather | bytes 278528 | tf_op jit(solution)/shard_map/all_gather | solution.py:35
  287.8 1.1 fusion.12
  288.9 0.0 all-gather.8.cloned.1.call-update
  288.9 0.0 copy-start.2
  288.9 0.0 reduce-scatter.8.cloned.1.call-start
  289.0 38.6 %all-gather.8.cloned.1.call-done = bf16[128,8192]{1,0:T(8,128)(2,1)} async-done(((bf16[128,512]{1,0:T(8,128)(2,1)}), bf16[128,8192]{1,0:T(8,128)(2,1)}) %all-gather.8.cloned.1.call-update) | async-done | bytes 2097168 | tf_op jit(solution)/shard_map/all_gather | solution.py:37
  327.6 15.3 %fusion.16 = f32[128,1792]{1,0:T(8,128)S(1)} fusion(bf16[128,8192]{1,0:T(8,128)(2,1)} %all-gather.8.cloned.1.call-done, bf16[1792,8192]{1,0:T(8,128)(2,1)} %param.13), kind=kOutput, calls=%fused_computation.27 | convolution fusion | flops 3758096384 | bytes 32374784 | tf_op jit(solution)/shard_map/dot_general | solution.py:38
  342.8 0.0 copy-done.2
  342.8 14.4 %fusion.5 = f32[128,8192]{1,0:T(8,128)S(1)} fusion(bf16[8192,1792]{1,0:T(8,128)(2,1)} %param.11, f32[128,1792]{1,0:T(8,128)S(1)} %fusion.16, f32[128,1792]{1,0:T(8,128)} %fusion.14, f32[128,1792]{1,0:T(8,128)S(1)} %copy-done.2), kind=kOutput, calls=%fused_computation.14 | convolution fusion | flops 3760390144 | bytes 36306944 | tf_op jit(solution)/shard_map/dot_general | solution.py:41
  357.3 16.8 %convolution_add_fusion = f32[128,8192]{1,0:T(8,128)} fusion(f32[128,8192]{1,0:T(8,128)S(1)} %fusion.5, bf16[8192,1792]{1,0:T(8,128)(2,1)} %param.12, f32[128,1792]{1,0:T(8,128)S(1)} %fusion.16, f32[128,1792]{1,0:T(8,128)S(1)} %copy-done.2), kind=kOutput, calls=%fused_computation.1 | convolution fusion | flops 3760521216 | bytes 39583744 | tf_op jit(solution)/shard_map/dot_general | solution.py:42
  374.1 1.7 add_dynamic-update-slice_fusion
  375.8 0.0 reduce-scatter.8.cloned.1.call-update
  375.8 71.5 %reduce-scatter.8.cloned.1.call-done = f32[8,8192]{1,0:T(8,128)} async-done(((f32[128,8192]{1,0:T(8,128)}), f32[8,8192]{1,0:T(8,128)}) %reduce-scatter.8.cloned.1.call-update) | async-done | bytes 262160 | tf_op jit(solution)/shard_map/reduce_scatter | solution.py:44
  (3 shorter events, 0.0 us)
Async XLA Ops:
  6.5 200.4 %copy-start = (bf16[512,1024]{1,0:T(8,128)(2,1)S(1)}, bf16[512,1024]{1,0:T(8,128)(2,1)}, u32[]{:S(2)}) copy-start(bf16[512,1024]{1,0:T(8,128)(2,1)} %param.14) | copy-start | bytes 3145732
  6.5 47.1 %all-gather.4.cloned.1.call-start = ((), (), s32[]{:S(2)}) async-start(), calls=%async_computation.3 | async-start | bytes 2228224 | tf_op jit(solution)/shard_map/all_gather | solution.py:11
  7.3 88.8 %all-gather.6.cloned.1.call-start = ((), (), s32[]{:S(2)}) async-start(), calls=%async_computation.4 | async-start | bytes 2228224 | tf_op jit(solution)/shard_map/all_gather | solution.py:12
  8.0 198.9 %reduce-scatter.6.cloned.1.call-start = ((), (), s32[]{:S(2)}) async-start(), calls=%async_computation.5 | async-start | bytes 4456448 | tf_op jit(solution)/shard_map/reduce_scatter | solution.py:28
  53.7 15.2 %copy-start.3 = (bf16[128,8192]{1,0:T(8,128)(2,1)S(1)}, bf16[128,8192]{1,0:T(8,128)(2,1)}, u32[]{:S(2)}) copy-start(bf16[128,8192]{1,0:T(8,128)(2,1)} %all-gather.4.cloned.1.call-done) | copy-start | bytes 6291460
  96.0 15.6 %copy-start.1 = (bf16[128,8192]{1,0:T(8,128)(2,1)S(1)}, bf16[128,8192]{1,0:T(8,128)(2,1)}, u32[]{:S(2)}) copy-start(bf16[128,8192]{1,0:T(8,128)(2,1)} %all-gather.6.cloned.1.call-done) | copy-start | bytes 6291460
  135.7 131.0 %reduce-scatter.10.cloned.1.call-start = ((), (), s32[]{:S(2)}) async-start(), calls=%async_computation.8 | async-start | bytes 557056
  211.6 15.8 %copy-start.4 = (s32[128]{0:T(128)S(1)}, s32[128]{0:T(128)}, u32[]{:S(2)}) copy-start(s32[128]{0:T(128)} %param.10) | copy-start | bytes 1540
  211.7 115.9 %all-gather.8.cloned.1.call-start = ((), (), s32[]{:S(2)}) async-start(), calls=%async_computation.6 | async-start | bytes 2228224 | tf_op jit(solution)/shard_map/all_gather | solution.py:37
  288.9 53.9 %copy-start.2 = (f32[128,1792]{1,0:T(8,128)S(1)}, f32[128,1792]{1,0:T(8,128)}, u32[]{:S(2)}) copy-start(f32[128,1792]{1,0:T(8,128)} %fusion.13) | copy-start | bytes 2752516
  288.9 158.4 %reduce-scatter.8.cloned.1.call-start = ((), (), s32[]{:S(2)}) async-start(), calls=%async_computation.7 | async-start | bytes 4456448 | tf_op jit(solution)/shard_map/reduce_scatter | solution.py:44
Sparse Core Ops, SparseCore 0:
  9.5 44.0 all-gather.3
  55.8 40.1 all-gather.5
  135.8 71.0 reduce-scatter.5
  211.8 54.8 reduce-scatter.9
  289.1 38.4 all-gather.7
  376.0 71.2 reduce-scatter.7
where the time goes:
time: 455 us; the launch traced here: 454 us
  waiting for transfers between devices  274 us (60%)
  matrix products  118 us (26%)
  local copies, waits for them, and re-layouts  27.2 us (6%)
  blocking collectives  20.1 us (4%)
  between operations  13.6 us (3%)
    reduce_scatter x1, waiting for transfers between devices, on_device(): lax.psum_scatter(lax.dynamic_update_slice_in_dim(result, current + cot_co...  71.5 us
    reduce_scatter x1, waiting for transfers between devices, on_device(): lax.psum_scatter(partial_value, 'tensor', scatter_dimension=1, tiled=True)  71.2 us
    all_gather x1, waiting for transfers between devices, on_device(): lax.all_gather(inputs, 'tensor', axis=0, tiled=True)  45.6 us
    all_gather x1, waiting for transfers between devices, on_device(): lax.all_gather(cot_cols.astype(jnp.bfloat16), 'tensor', axis=1, tiled=True)  38.6 us
    unnamed x7, waiting for transfers between devices  32.2 us
    dot_general x1, matrix products, on_device(): jnp.dot(tan_hidden, down_weight, preferred_element_type=jnp.float32)  24 us
    all_gather x1, blocking collectives, on_device(): weighted = lax.all_gather(weighted_cols, 'tensor', axis=1, tiled=True)  20.1 us
    unnamed x13, local copies, waits for them, and re-layouts  18.7 us
  transfers between devices with their start and end apart: 6, of which 6 were waited for; matrix products, arithmetic and copies ran while one was open for 11% of the time, Pallas kernels for 0%

commit v1 on v0

v1 whole, which is shorter than its diff:
```python
import functools

import jax
import jax.numpy as jnp
from jax import lax
from jax.experimental import pallas as pl
from jax.experimental.pallas import tpu as pltpu
from jax.sharding import PartitionSpec as P

F32 = jnp.float32
BF16 = jnp.bfloat16
NZ, NX, NC = 4, 2, 2
MESH = pl.DeviceIdType.MESH
VMEM = pltpu.VMEM
DMA = pltpu.SemaphoreType.DMA
LIMIT = 62 << 20


def place():
    me = lax.axis_index("tensor")
    return me, me // 4, (me // 2) % 2, me % 2


def index_of(z, x, c):
    return (z % NZ) * 4 + x * 2 + c


def greet(z, x, c):
    barrier = pltpu.get_barrier_semaphore()
    others = [index_of(z + k, x, c) for k in (1, 2, 3)]
    others += [index_of(z, 1 - x, c), index_of(z, x, 1 - c)]
    for other in others:
        pl.semaphore_signal(barrier, inc=1, device_id={"tensor": other}, device_id_type=MESH)
    pl.semaphore_wait(barrier, 5)


def remote(src, dst, send, recv, other):
    return pltpu.make_async_remote_copy(
        src_ref=src,
        dst_ref=dst,
        send_sem=send,
        recv_sem=recv,
        device_id={"tensor": other},
        device_id_type=MESH,
    )


def span(start, size):
    return pl.ds(pl.multiple_of(start, size), size)


def loop(lo, hi, body):
    def step(i, carry):
        body(i)
        return carry

    lax.fori_loop(lo, hi, step, 0)


def nt(a, b):
    return lax.dot_general(a, b, (((1,), (1,)), ((), ())), preferred_element_type=F32)


def nn(a, b):
    return jnp.dot(a, b, preferred_element_type=F32)


def forward_kernel(
    nf, fc, slots, feat,
    xv_ref, gate_ref, up_ref, th_ref, cg_ref, ca_ref, vc_ref,
    xg, wg, wu, acc_g, acc_u, wsem, zs, zr, xs, xr, cs, cr,
):
    me, z, x, c = place()
    hidden = th_ref.shape[1]

    def weights(f):
        slot = lax.rem(f, slots)
        rows = span(f * fc, fc)
        return (
            pltpu.make_async_copy(gate_ref.at[rows], wg.at[slot], wsem.at[0, slot]),
            pltpu.make_async_copy(up_ref.at[rows], wu.at[slot], wsem.at[1, slot]),
        )

    def fetch(f):
        for copy in weights(f):
            copy.start()

    loop(0, slots, fetch)
    slot_me = (c * NX + x) * NZ + z
    mine = span(slot_me * 16, 16)
    xg[mine, :] = xv_ref[...]
    greet(z, x, c)

    def send_z(f, k):
        cols = span(f * fc, fc)
        return remote(
            xv_ref.at[:, cols], xg.at[mine, cols], zs.at[f, k - 1], zr.at[f, k - 1],
            index_of(z + k, x, c),
        )

    def send_x(f):
        part = xg.at[span((c * NX + x) * 64, 64), span(f * fc, fc)]
        return remote(part, part, xs.at[f], xr.at[f], index_of(z, 1 - x, c))

    def send_c(f):
        part = xg.at[span(c * 128, 128), span(f * fc, fc)]
        return remote(part, part, cs.at[f], cr.at[f], index_of(z, x, 1 - c))

    def first(f):
        for k in (1, 2, 3):
            send_z(f, k).start()

    loop(0, nf, first)
    acc_g[...] = jnp.zeros_like(acc_g)
    acc_u[...] = jnp.zeros_like(acc_u)

    def step(s):
        @pl.when(s < nf)
        def _():
            for k in (1, 2, 3):
                send_z(s, k).wait_recv()
            send_x(s).start()

        @pl.when((s >= 1) & (s <= nf))
        def _():
            send_x(s - 1).wait_recv()
            send_c(s - 1).start()

        @pl.when(s >= 2)
        def _():
            f = s - 2
            send_c(f).wait_recv()
            for copy in weights(f):
                copy.wait()
            slot = lax.rem(f, slots)
            block = xg[:, span(f * fc, fc)]
            acc_g[...] += nn(block, wg[slot])
            acc_u[...] += nn(block, wu[slot])

            @pl.when(f + slots < nf)
            def _():
                fetch(f + slots)

    loop(0, nf + 2, step)

    tile = 256

    def finish(t):
        cols = span(t * tile, tile)
        both_g = acc_g[:, cols].reshape(16, 2, 8, tile)
        both_u = acc_u[:, cols].reshape(16, 2, 8, tile)
        pre_gate, tan_gate = both_g[:, 0].reshape(128, tile), both_g[:, 1].reshape(128, tile)
        pre_up, tan_up = both_u[:, 0].reshape(128, tile), both_u[:, 1].reshape(128, tile)
        sig = jax.nn.sigmoid(pre_gate)
        act = pre_gate * sig
        slope = sig * (1.0 + pre_gate * (1.0 - sig))
        coef = pre_up * slope
        th_ref[:, cols] = (slope * tan_gate * pre_up + act * tan_up).astype(BF16)
        cg_ref[:, cols] = coef
        ca_ref[:, cols] = act

    loop(0, hidden // tile, finish)
    own = xg[:, span(me * feat, feat)].astype(F32).reshape(16, 2, 8, feat)
    vc_ref[...] = own[:, 1].reshape(128, feat)

    def drain(f):
        for k in (1, 2, 3):
            send_z(f, k).wait_send()
        send_x(f).wait_send()
        send_c(f).wait_send()

    loop(0, nf, drain)


def middle_kernel(
    th_ref, cg_ref, ca_ref, vc_ref, sk_ref, prec_ref, down_ref,
    bg_ref, bu_ref, cot_ref,
    dn, pbuf, rb, xsb, xrb, zsb, zrb, sk, rc, sxs, sxr, szs, szr, wga, cga, accb,
    dsem, s_send, s_recv, k_send, k_recv, w_send, w_recv, a_send, a_recv,
):
    me, z, x, c = place()
    x_peer, c_peer = index_of(z, 1 - x, c), index_of(z, x, 1 - c)
    width = pbuf.shape[2]
    feat = width // 4

    def weights(i):
        cols = span(((z + 1 + i) % NZ) * width, width)
        return pltpu.make_async_copy(down_ref.at[:, cols], dn.at[i], dsem.at[i])

    loop(0, NZ, lambda i: weights(i).start())
    greet(z, x, c)

    def cols_of(xx, cc):
        return span((xx * 2 + cc) * feat, feat)

    def rs_c(i, xx):
        return remote(
            pbuf.at[i, :, cols_of(xx, 1 - c)], rb.at[i, xx],
            s_send.at[i, xx], s_recv.at[i, xx], c_peer,
        )

    def rs_x(i):
        return remote(xsb.at[i], xrb.at[i], s_send.at[i, 2], s_recv.at[i, 2], x_peer)

    def rs_z(i):
        return remote(
            zsb.at[i], zrb.at[i], s_send.at[i, 3], s_recv.at[i, 3], index_of(z + 1 + i, x, c)
        )

    def step(s):
        @pl.when(s < NZ)
        def _():
            weights(s).wait()

            def tile(t):
                cols = span(t * feat, feat)
                pbuf[s, :, cols] = nn(th_ref[...], dn[s, :, cols])

            loop(0, 4, tile)
            rs_c(s, 0).start()
            rs_c(s, 1).start()

        @pl.when((s >= 1) & (s <= NZ))
        def _():
            i = s - 1
            rs_c(i, 0).wait_recv()
            rs_c(i, 1).wait_recv()
            xsb[i] = (pbuf[i, :, cols_of(1 - x, c)] + rb[i, 1 - x]).astype(BF16)
            rs_x(i).start()

        @pl.when((s >= 2) & (s <= NZ))
        def _():
            i = s - 2
            rs_x(i).wait_recv()
            total = pbuf[i, :, cols_of(x, c)] + rb[i, x] + xrb[i].astype(F32)
            zsb[i] = total.astype(BF16)
            rs_z(i).start()

    loop(0, NZ + 1, step)
    last = NZ - 1
    rs_x(last).wait_recv()
    total = pbuf[last, :, cols_of(x, c)] + rb[last, x] + xrb[last].astype(F32) + vc_ref[...]
    for i in range(NZ - 1):
        rs_z(i).wait_recv()
        total = total + zrb[i].astype(F32)

    high = total.astype(BF16)
    low = (total - high.astype(F32)).astype(BF16)
    part = nn(high, sk_ref[...]) + nn(low, sk_ref[...])
    sk[...] = part.T.reshape(sk.shape)
    copy_c = remote(sk.at[:, :, 1 - c], rc, k_send.at[0], k_recv.at[0], c_peer)
    copy_c.start()
    copy_c.wait_recv()
    sxs[...] = sk[:, 1 - x, c] + rc[:, 1 - x]
    copy_x = remote(sxs, sxr, k_send.at[1], k_recv.at[1], x_peer)
    copy_x.start()
    copy_x.wait_recv()
    szs[...] = sk[:, x, c] + rc[:, x] + sxr[...]
    copies = [
        remote(szs.at[(z + k) % NZ], szr.at[k - 1], k_send.at[1 + k], k_recv.at[1 + k],
               index_of(z + k, x, c))
        for k in (1, 2, 3)
    ]
    for copy in copies:
        copy.start()
    value = szs[z]
    for k, copy in enumerate(copies):
        copy.wait_recv()
        value = value + szr[k]
    for copy in copies + [copy_c, copy_x]:
        copy.wait_send()

    wga[z, x, c] = (prec_ref[...] * value).astype(BF16)
    mine = wga.at[z, x, c]
    copies = [
        remote(mine, mine, w_send.at[k - 1], w_recv.at[k - 1], index_of(z + k, x, c))
        for k in (1, 2, 3)
    ]
    for copy in copies:
        copy.start()
    for copy in copies:
        copy.wait_recv()
    copy_x = remote(wga.at[:, x, c], wga.at[:, x, c], w_send.at[3], w_recv.at[3], x_peer)
    copy_x.start()
    copy_x.wait_recv()
    copy_c = remote(wga.at[:, :, c], wga.at[:, :, c], w_send.at[4], w_recv.at[4], c_peer)
    copy_c.start()
    copy_c.wait_recv()
    for copy in copies + [copy_x, copy_c]:
        copy.wait_send()
    flat = wga[...].reshape(-1, 128).astype(F32).T.astype(BF16)
    cot = nt(flat, sk_ref[...])
    cot_ref[...] = cot

    cga[z, x, c] = cot.astype(BF16)

    def ag_z(k):
        part = cga.at[z, x, c]
        return remote(part, part, a_send.at[0, k], a_recv.at[0, k], index_of(z + k, x, c))

    def ag_x(k):
        part = cga.at[(z + NZ - k) % NZ, x, c]
        return remote(part, part, a_send.at[1, k], a_recv.at[1, k], x_peer)

    def ag_c(k, own):
        part = cga.at[(z + NZ - k) % NZ, x if own else 1 - x, c]
        row = 2 if own else 3
        return remote(part, part, a_send.at[row, k], a_recv.at[row, k], c_peer)

    def ag_c_other(k, own):
        return ag_c(k, own)

    def use(k, xx, cc):
        accb[...] += nt(cga[(z + NZ - k) % NZ, xx, cc], dn[3 - k, :, cols_of(xx, cc)])

    for k in (1, 2, 3):
        ag_z(k).start()
    accb[...] = jnp.zeros_like(accb)

    def own_column(k):
        @pl.when(k >= 1)
        def _():
            ag_z(k).wait_recv()

        ag_x(k).start()
        ag_c(k, True).start()
        use(k, x, c)

    loop(0, NZ, own_column)

    def other_column(k):
        ag_x(k).wait_recv()
        ag_c(k, False).start()
        use(k, 1 - x, c)

    loop(0, NZ, other_column)

    def sibling_own(k):
        ag_c_other(k, True).wait_recv()
        use(k, x, 1 - c)

    loop(0, NZ, sibling_own)

    def sibling_other(k):
        ag_c_other(k, False).wait_recv()
        use(k, 1 - x, 1 - c)

    loop(0, NZ, sibling_other)

    bg_ref[...] = (accb[...] * cg_ref[...]).astype(BF16)
    bu_ref[...] = (accb[...] * ca_ref[...]).astype(BF16)

    def drain(k):
        @pl.when(k >= 1)
        def _():
            ag_z(k).wait_send()
            rs_z(k - 1).wait_send()

        ag_x(k).wait_send()
        ag_c(k, True).wait_send()
        ag_c(k, False).wait_send()
        rs_c(k, 0).wait_send()
        rs_c(k, 1).wait_send()
        rs_x(k).wait_send()

    loop(0, NZ, drain)


def final_kernel(
    nf, fc, slots,
    bg_ref, bu_ref, cot_ref, gate_ref, up_ref, out_ref,
    wg, wu, pbuf, rb, xsb, xrb, tb, zsb, zrb, wsem, c_send, c_recv, x_send, x_recv, z_send, z_recv,
):
    me, z, x, c = place()
    x_peer, c_peer = index_of(z, 1 - x, c), index_of(z, x, 1 - c)
    feat = cot_ref.shape[1]
    half = fc // 2

    def weights(f):
        slot = lax.rem(f, slots)
        rows = span(f * fc, fc)
        return (
            pltpu.make_async_copy(gate_ref.at[rows], wg.at[slot], wsem.at[0, slot]),
            pltpu.make_async_copy(up_ref.at[rows], wu.at[slot], wsem.at[1, slot]),
        )

    def fetch(f):
        for copy in weights(f):
            copy.start()

    loop(0, slots, fetch)
    greet(z, x, c)

    def rs_c(f):
        return remote(
            pbuf.at[f, span((1 - c) * 64, 64)], rb.at[f], c_send.at[f], c_recv.at[f], c_peer
        )

    def rs_x(f):
        return remote(xsb.at[f], xrb.at[f], x_send.at[f], x_recv.at[f], x_peer)

    def rs_z(f, k):
        return remote(
            zsb.at[f, k - 1], zrb.at[f, k - 1], z_send.at[f, k - 1], z_recv.at[f, k - 1],
            index_of(z + k, x, c),
        )

    def step(s):
        @pl.when(s < nf)
        def _():
            for copy in weights(s):
                copy.wait()
            slot = lax.rem(s, slots)
            pbuf[s] = nt(bg_ref[...], wg[slot]) + nt(bu_ref[...], wu[slot])

            @pl.when(s == (me * feat) // fc)
            def _():
                cols = span(((me * feat) % fc) // feat * feat, feat)
                pbuf[s, :, cols] += cot_ref[...]

            rs_c(s).start()

            @pl.when(s + slots < nf)
            def _():
                fetch(s + slots)

        @pl.when((s >= 1) & (s <= nf))
        def _():
            f = s - 1
            rs_c(f).wait_recv()
            away = pbuf[f, span(c * 64 + (1 - x) * 32, 32)] + rb[f, span((1 - x) * 32, 32)]
            xsb[f] = away.astype(BF16)
            rs_x(f).start()

        @pl.when((s >= 2) & (s <= nf + 1))
        def _():
            f = s - 2
            rs_x(f).wait_recv()
            tb[...] = (
                pbuf[f, span(c * 64 + x * 32, 32)]
                + rb[f, span(x * 32, 32)]
                + xrb[f].astype(F32)
            )
            for k in (1, 2, 3):
                rows = tb[span(((z + k) % NZ) * 8, 8), :]
                folded = jnp.concatenate([rows[:, :half], rows[:, half:]], axis=0)
                zsb[f, k - 1] = folded.astype(BF16)
                rs_z(f, k).start()
            out_ref[:, span(f * fc, fc)] = tb[span(z * 8, 8), :]

        @pl.when(s >= 3)
        def _():
            f = s - 3
            total = out_ref[:, span(f * fc, fc)]
            for k in (1, 2, 3):
                rs_z(f, k).wait_recv()
                folded = zrb[f, k - 1].astype(F32)
                total = total + jnp.concatenate([folded[:8], folded[8:]], axis=1)
            out_ref[:, span(f * fc, fc)] = total

    loop(0, nf + 3, step)

    def drain(f):
        rs_c(f).wait_send()
        rs_x(f).wait_send()
        for k in (1, 2, 3):
            rs_z(f, k).wait_send()

    loop(0, nf, drain)


def rows_kernel(depth, ids_ref, table_ref, out_ref, buf, sem):
    count = out_ref.shape[1]

    def copy(t):
        slot = lax.rem(t, depth)
        block = pl.multiple_of(lax.shift_right_logical(ids_ref[t], 7) * 128, 128)
        return pltpu.make_async_copy(table_ref.at[:, pl.ds(block, 128)], buf.at[slot], sem.at[slot])

    loop(0, depth, lambda t: copy(t).start())
    lanes = lax.broadcasted_iota(jnp.int32, out_ref.shape, 1)

    def step(t, held):
        copy(t).wait()
        block = buf[lax.rem(t, depth)].astype(F32)
        shift = jnp.bitwise_and(t + 128 - jnp.bitwise_and(ids_ref[t], 127), 127)
        held = jnp.where(lanes == t, pltpu.roll(block, shift, axis=1), held)

        @pl.when(t + depth < count)
        def _():
            copy(t + depth).start()

        return held

    out_ref[...] = lax.fori_loop(0, count, step, jnp.zeros(out_ref.shape, F32))


ANY = pl.BlockSpec(memory_space=pl.ANY)
IN_VMEM = pl.BlockSpec(memory_space=pltpu.VMEM)


def params(collective_id):
    return pltpu.CompilerParams(
        collective_id=collective_id, has_side_effects=True, vmem_limit_bytes=LIMIT
    )


def cost(flops, nbytes):
    return pl.CostEstimate(flops=flops, bytes_accessed=nbytes, transcendentals=0)


def fast(inputs, tangent, token_ids, gate_weight, up_weight, down_weight, sketch, teacher_precision):
    model, hidden = gate_weight.shape
    feat, rank = sketch.shape
    coords = teacher_precision.shape[1]
    rows = token_ids.shape[0]
    fc = 1024
    nf = model // fc
    shape = jax.ShapeDtypeStruct

    depth = 32
    order = token_ids.reshape(NZ, NX, NC, 8).transpose(2, 1, 0, 3).reshape(rows)
    prec = pl.pallas_call(
        functools.partial(rows_kernel, depth),
        out_shape=shape((coords, rows), F32),
        in_specs=[pl.BlockSpec(memory_space=pltpu.SMEM), ANY],
        out_specs=IN_VMEM,
        scratch_shapes=[VMEM((depth, coords, 128), BF16), DMA((depth,))],
        name="precision_rows",
    )(order, teacher_precision.T)

    slots = 3
    xv = jnp.concatenate([inputs, tangent], axis=0)
    th, cg, ca, vc = pl.pallas_call(
        functools.partial(forward_kernel, nf, fc, slots, feat),
        out_shape=[
            shape((rows, hidden), BF16),
            shape((rows, hidden), F32),
            shape((rows, hidden), F32),
            shape((rows, feat), F32),
        ],
        in_specs=[IN_VMEM, ANY, ANY],
        out_specs=[IN_VMEM] * 4,
        scratch_shapes=[
            VMEM((2 * rows, model), BF16),
            VMEM((slots, fc, hidden), BF16),
            VMEM((slots, fc, hidden), BF16),
            VMEM((2 * rows, hidden), F32),
            VMEM((2 * rows, hidden), F32),
            DMA((2, slots)),
            DMA((nf, 3)), DMA((nf, 3)),
            DMA((nf,)), DMA((nf,)),
            DMA((nf,)), DMA((nf,)),
        ],
        compiler_params=params(0),
        cost_estimate=cost(8 * rows * model * hidden, 4 * model * hidden),
        name="gather_forward",
    )(xv, gate_weight, up_weight)

    width = model // NZ
    bg, bu, cot = pl.pallas_call(
        middle_kernel,
        out_shape=[shape((rows, hidden), BF16), shape((rows, hidden), BF16), shape((rows, feat), F32)],
        in_specs=[IN_VMEM] * 6 + [ANY],
        out_specs=[IN_VMEM] * 3,
        scratch_shapes=[
            VMEM((NZ, hidden, width), BF16),
            VMEM((NZ, rows, width), F32),
            VMEM((NZ, 2, rows, feat), F32),
            VMEM((NZ, rows, feat), BF16), VMEM((NZ, rows, feat), BF16),
            VMEM((3, rows, feat), BF16), VMEM((3, rows, feat), BF16),
            VMEM((NZ, NX, NC, coords, rows), F32),
            VMEM((NZ, NX, coords, rows), F32),
            VMEM((NZ, coords, rows), F32), VMEM((NZ, coords, rows), F32),
            VMEM((NZ, coords, rows), F32), VMEM((3, coords, rows), F32),
            VMEM((NZ, NX, NC, coords, rows), BF16),
            VMEM((NZ, NX, NC, rows, feat), BF16),
            VMEM((rows, hidden), F32),
            DMA((NZ,)),
            DMA((NZ, 4)), DMA((NZ, 4)),
            DMA((5,)), DMA((5,)),
            DMA((5,)), DMA((5,)),
            DMA((4, NZ)), DMA((4, NZ)),
        ],
        compiler_params=params(1),
        cost_estimate=cost(4 * rows * model * hidden, 2 * model * hidden),
        name="down_sketch_back",
    )(th, cg, ca, vc, sketch, prec, down_weight)

    return pl.pallas_call(
        functools.partial(final_kernel, nf, fc, slots),
        out_shape=shape((8, model), F32),
        in_specs=[IN_VMEM] * 3 + [ANY, ANY],
        out_specs=IN_VMEM,
        scratch_shapes=[
            VMEM((slots, fc, hidden), BF16),
            VMEM((slots, fc, hidden), BF16),
            VMEM((nf, rows, fc), F32),
            VMEM((nf, 64, fc), F32),
            VMEM((nf, 32, fc), BF16), VMEM((nf, 32, fc), BF16),
            VMEM((32, fc), F32),
            VMEM((nf, 3, 16, fc // 2), BF16), VMEM((nf, 3, 16, fc // 2), BF16),
            DMA((2, slots)),
            DMA((nf,)), DMA((nf,)),
            DMA((nf,)), DMA((nf,)),
            DMA((nf, 3)), DMA((nf, 3)),
        ],
        compiler_params=params(2),
        cost_estimate=cost(4 * rows * model * hidden, 4 * model * hidden),
        name="backward_scatter",
    )(bg, bu, cot, gate_weight, up_weight)


def general(inputs, tangent, token_ids, gate_weight, up_weight, down_weight, sketch, teacher_precision):
    rows_x, rows_v = (
        lax.all_gather(inputs, "tensor", axis=0, tiled=True),
        lax.all_gather(tangent, "tensor", axis=0, tiled=True),
    )
    position = lax.axis_index("tensor")
    feat_local = sketch.shape[0]
    offset = position * feat_local
    pre_gate = jnp.dot(rows_x, gate_weight, preferred_element_type=F32)
    pre_up = jnp.dot(rows_x, up_weight, preferred_element_type=F32)
    tan_gate = jnp.dot(rows_v, gate_weight, preferred_element_type=F32)
    tan_up = jnp.dot(rows_v, up_weight, preferred_element_type=F32)
    sig = jax.nn.sigmoid(pre_gate)
    act = pre_gate * sig
    slope = sig * (1.0 + pre_gate * (1.0 - sig))
    tan_hidden = (slope * tan_gate * pre_up + act * tan_up).astype(BF16)
    v_mine = lax.dynamic_slice_in_dim(rows_v, offset, feat_local, 1)
    own_term = jnp.dot(v_mine, sketch, preferred_element_type=F32)
    partial_value = jnp.dot(tan_hidden, down_weight, preferred_element_type=F32)
    summed_cols = lax.psum_scatter(partial_value, "tensor", scatter_dimension=1, tiled=True)
    sketch_part = (
        jnp.dot(summed_cols, sketch.astype(F32), precision=lax.Precision.HIGHEST) + own_term
    )
    sketch_cols = lax.psum_scatter(sketch_part, "tensor", scatter_dimension=1, tiled=True)
    rows_prec = teacher_precision[token_ids].astype(F32)
    weighted_cols = (rows_prec * sketch_cols).astype(BF16)
    weighted = lax.all_gather(weighted_cols, "tensor", axis=1, tiled=True)
    cot_cols = jnp.dot(weighted, sketch.T, preferred_element_type=F32)
    cot_full = lax.all_gather(cot_cols.astype(BF16), "tensor", axis=1, tiled=True)
    back_hidden = jnp.dot(cot_full, down_weight.T, preferred_element_type=F32)
    back_gate = (back_hidden * pre_up * slope).astype(BF16)
    back_up = (back_hidden * act).astype(BF16)
    result = jnp.dot(back_gate, gate_weight.T, preferred_element_type=F32)
    result = result + jnp.dot(back_up, up_weight.T, preferred_element_type=F32)
    current = lax.dynamic_slice_in_dim(result, offset, feat_local, 1)
    return lax.psum_scatter(
        lax.dynamic_update_slice_in_dim(result, current + cot_cols, offset, 1),
        "tensor",
        scatter_dimension=0,
        tiled=True,
    )


def solution(mesh):
    on_device = fast if mesh.shape["tensor"] == NZ * NX * NC else general
    return jax.shard_map(
        on_device,
        mesh=mesh,
        in_specs=(
            P(("groups", "tensor"), None),
            P(("groups", "tensor"), None),
            P("groups"),
            P(None, "tensor"),
            P(None, "tensor"),
            P("tensor", None),
            P("tensor", None),
            P(None, "tensor"),
        ),
        out_specs=P(("groups", "tensor"), None),
        check_vma=False,
    )
```

time: 455 us -> 180 us (0.40)
  waiting for transfers between devices: 274 us -> 0 us
  Pallas kernels: 0 us -> 175 us
  matrix products: 118 us -> 0 us
  local copies, waits for them, and re-layouts: 27.2 us -> 3.03 us
  blocking collectives: 20.1 us -> 0 us
  between operations: 13.6 us -> 0.05 us
    pallas_call x0 -> x4, Pallas kernels: none -> 175 us  [the longest x1 73.1 us: fast(): pl.pallas_call(middle_kernel, out_shape=[shape((rows, hidden), BF16), sha...]
    reduce_scatter x2 -> x0, waiting for transfers between devices: 143 us -> none  [the longest x1 71.5 us: on_device(): lax.psum_scatter(lax.dynamic_update_slice_in_dim(result, current + cot_co...]
    dot_general x10 -> x0, matrix products: 118 us -> none  [the longest x1 24 us: on_device(): jnp.dot(tan_hidden, down_weight, preferred_element_type=jnp.float32)]
    all_gather x3 -> x0, waiting for transfers between devices: 98.9 us -> none  [the longest x1 45.6 us: on_device(): lax.all_gather(inputs, 'tensor', axis=0, tiled=True)]
    unnamed x7 -> x0, waiting for transfers between devices: 32.2 us -> none
    all_gather x1 -> x0, blocking collectives: 20.1 us -> none  [on_device(): weighted = lax.all_gather(weighted_cols, 'tensor', axis=1, tiled=True)]
    unnamed x13 -> x1, local copies, waits for them, and re-layouts: 18.7 us -> 1.67 us
    gather x1 -> x0, local copies, waits for them, and re-layouts: 8.47 us -> none  [on_device(): rows_prec = teacher_precision[token_ids].astype(jnp.float32)]
  transfers between devices with their start and end apart: 6 -> 0, of which waited for: 6 -> 0; matrix products, arithmetic and copies ran while one was open for 11% -> 0% of each run, Pallas kernels for 0% -> 0%
where the time goes in v1:
time: 180 us
  Pallas kernels  175 us (97%)
  local copies, waits for them, and re-layouts  3.03 us (2%)
    pallas_call x1, Pallas kernels, fast(): pl.pallas_call(middle_kernel, out_shape=[shape((rows, hidden), BF16), sha...  73.1 us
    pallas_call x1, Pallas kernels, fast(): pl.pallas_call(functools.partial(forward_kernel, nf, fc, slots, feat), ou...  48.5 us
    pallas_call x1, Pallas kernels, fast(): pl.pallas_call(functools.partial(final_kernel, nf, fc, slots), out_shape=...  41.8 us
    pallas_call x1, Pallas kernels, fast(): pl.pallas_call(functools.partial(rows_kernel, depth), out_shape=shape((co...  11.9 us

profile of v1, /device:TPU:0, one launch (start us, length us, event | category | flops | bytes accessed | tf_op | source)
XLA Modules:
  0.0 180.0 jit_solution(4451948620610355121)
XLA Ops:
  0.0 0.7 reshape.6
  0.8 0.6 reshape.7.ids_ref
  1.4 11.9 %precision_rows.1.prec_ref = f32[64,128]{1,0:T(8,128)} custom-call(s32[128]{0:T(128)} %reshape.7.ids_ref, bf16[64,64128]{1,0:T(8,128)(2,1)} %bitcast.2), custom_call_target="tpu_custom_call" | custom-call | tf_op jit(solution)/shard_map/precision_rows/pallas_call | solution.py:523
  13.3 1.7 pad_maximum_fusion.xv_ref
  15.0 48.5 %gather_forward.1 = (bf16[128,1792]{1,0:T(8,128)(2,1)}, f32[128,1792]{1,0:T(8,128)}, f32[128,1792]{1,0:T(8,128)}, f32[128,512]{1,0:T(8,128)}) custom-call(bf16[16,8192]{1,0:T(8,128)(2,1)} %pad_maximum_fusion.xv_ref, bf16[8192,1792]{1,0:T(8,128)(2,1)} %gate_ref.3, bf16[8192,1792]{1,0:T(8,128)(2,1)} %up_ref.3), custom_call_target="tpu_custom_call" | custom-call | flops 15032385536 | bytes 58720256 | tf_op jit(solution)/shard_map/gather_forward/pallas_call | solution.py:534
  63.5 73.1 %down_sketch_back.1 = (bf16[128,1792]{1,0:T(8,128)(2,1)}, bf16[128,1792]{1,0:T(8,128)(2,1)}, f32[128,512]{1,0:T(8,128)}) custom-call(bf16[128,1792]{1,0:T(8,128)(2,1)} %get-tuple-element.12.th_ref, f32[128,1792]{1,0:T(8,128)} %get-tuple-element.13.cg_ref, f32[128,1792]{1,0:T(8,128)} %get-tuple-element.14.ca_ref, f32[128,512]{1,0:T(8,128)} %get-tuple-element.15.vc_ref, ...), custom_call_target="tpu_custom_call" | custom-call | flops 7516192768 | bytes 29360128 | tf_op jit(solution)/shard_map/down_sketch_back/pallas_call | solution.py:561
  136.6 41.8 %backward_scatter.1 = f32[8,8192]{1,0:T(8,128)} custom-call(bf16[128,1792]{1,0:T(8,128)(2,1)} %get-tuple-element.16.bg_ref, bf16[128,1792]{1,0:T(8,128)(2,1)} %get-tuple-element.17.bu_ref, f32[128,512]{1,0:T(8,128)} %get-tuple-element.18.cot_ref, bf16[8192,1792]{1,0:T(8,128)(2,1)} %gate_ref.3, bf16[8192,1792]{1,0:T(8,128)(2,1)} %up_ref.3), custom_call_target="tpu_custom_call" | custom-call | flops 7516192768 | bytes 58720256 | tf_op jit(solution)/shard_map/backward_scatter/pallas_call | solution.py:590
  178.4 1.7 copy.11
  (1 shorter events, 0.0 us)

commit v2 on v1

v2 whole, which is shorter than its diff:
```python
import functools

import jax
import jax.numpy as jnp
from jax import lax
from jax.experimental import pallas as pl
from jax.experimental.pallas import tpu as pltpu
from jax.sharding import PartitionSpec as P

F32 = jnp.float32
BF16 = jnp.bfloat16
NZ, NX, NC = 4, 2, 2
MESH = pl.DeviceIdType.MESH
VMEM = pltpu.VMEM
DMA = pltpu.SemaphoreType.DMA
LIMIT = 62 << 20


def place():
    me = lax.axis_index("tensor")
    return me, me // 4, (me // 2) % 2, me % 2


def index_of(z, x, c):
    return (z % NZ) * 4 + x * 2 + c


def greet(z, x, c):
    barrier = pltpu.get_barrier_semaphore()
    others = [index_of(z + k, x, c) for k in (1, 2, 3)]
    others += [index_of(z, 1 - x, c), index_of(z, x, 1 - c)]
    for other in others:
        pl.semaphore_signal(barrier, inc=1, device_id={"tensor": other}, device_id_type=MESH)
    pl.semaphore_wait(barrier, 5)


def remote(src, dst, send, recv, other):
    return pltpu.make_async_remote_copy(
        src_ref=src,
        dst_ref=dst,
        send_sem=send,
        recv_sem=recv,
        device_id={"tensor": other},
        device_id_type=MESH,
    )


def span(start, size):
    return pl.ds(pl.multiple_of(start, size), size)


def loop(lo, hi, body):
    def step(i, carry):
        body(i)
        return carry

    lax.fori_loop(lo, hi, step, 0)


def nt(a, b):
    return lax.dot_general(a, b, (((1,), (1,)), ((), ())), preferred_element_type=F32)


def nn(a, b):
    return jnp.dot(a, b, preferred_element_type=F32)


def kernel(
    nf, fc, wc, slots, ahead, feat,
    in_ref, tan_ref, sk_ref, prec_ref, gate_ref, up_ref, down_ref, out_ref,
    xg, wg, wu, acc_g, acc_u, th, bu, vc, cot_own,
    dn, pbuf, rb, xsb, xrb, zsb, zrb, sk, rc, sxs, sxr, szs, szr, wga,
    bxs, bxr, bzs, bzr, tb,
    wsem, dsem, zs, zr, xs, xr, cs, cr,
    s_send, s_recv, k_send, k_recv, w_send, w_recv, a_send, a_recv,
    c_send, c_recv, x_send, x_recv, z_send, z_recv,
):
    me, z, x, c = place()
    x_peer, c_peer = index_of(z, 1 - x, c), index_of(z, x, 1 - c)
    hidden = th.shape[1]
    parts = fc // wc
    width = 4 * feat

    def weights(g):
        slot = lax.rem(g, slots)
        rows = span((g % (nf * parts)) * wc, wc)
        return (
            pltpu.make_async_copy(gate_ref.at[rows], wg.at[slot], wsem.at[0, slot]),
            pltpu.make_async_copy(up_ref.at[rows], wu.at[slot], wsem.at[1, slot]),
        )

    def fetch(g):
        for copy in weights(g):
            copy.start()

    def arrive(g):
        for copy in weights(g):
            copy.wait()

    def down(i):
        cols = span(((z + 1 + i) % NZ) * width, width)
        return pltpu.make_async_copy(down_ref.at[:, cols], dn.at[i], dsem.at[i])

    loop(0, slots, fetch)
    loop(0, NZ, lambda i: down(i).start())
    greet(z, x, c)


    slot_me = (c * NX + x) * NZ + z
    mine = span(slot_me * 16, 16)
    own = jnp.concatenate([in_ref[...].astype(F32), tan_ref[...].astype(F32)], axis=0)
    xg[mine, :] = own.astype(BF16)

    def gather_z(f, k):
        cols = span(f * fc, fc)
        return remote(
            xg.at[mine, cols], xg.at[mine, cols], zs.at[f, k - 1], zr.at[f, k - 1],
            index_of(z + k, x, c),
        )

    def gather_x(f, k):
        slot = (c * NX + x) * NZ + (z + NZ - k) % NZ
        part = xg.at[span(slot * 16, 16), span(f * fc, fc)]
        return remote(part, part, xs.at[f, k], xr.at[f, k], index_of(z, 1 - x, c))

    def gather_c(f):
        part = xg.at[span(c * 128, 128), span(f * fc, fc)]
        return remote(part, part, cs.at[f], cr.at[f], index_of(z, x, 1 - c))

    def first(f):
        for k in (1, 2, 3):
            gather_z(f, k).start()

    def first_x(f):
        gather_x(f, 0).start()

    first(0)
    first_x(0)
    loop(1, ahead, first)
    loop(1, nf, first_x)
    acc_g[...] = jnp.zeros_like(acc_g)
    acc_u[...] = jnp.zeros_like(acc_u)

    def forward_step(s):
        @pl.when(s < nf)
        def _():
            for k in (1, 2, 3):
                gather_z(s, k).wait_recv()
                gather_x(s, k).start()

            @pl.when(s + ahead < nf)
            def _():
                first(s + ahead)

        @pl.when((s >= 1) & (s <= nf))
        def _():
            for k in range(NZ):
                gather_x(s - 1, k).wait_recv()
            gather_c(s - 1).start()

        @pl.when(s >= 2)
        def _():
            f = s - 2
            gather_c(f).wait_recv()

            def piece(h):
                g = f * parts + h
                arrive(g)
                slot = lax.rem(g, slots)
                block = xg[:, span(g * wc, wc)]
                acc_g[...] += nn(block, wg[slot])
                acc_u[...] += nn(block, wu[slot])
                fetch(g + slots)

            loop(0, parts, piece)

    loop(0, nf + 2, forward_step)

    tile = 256

    def finish(t):
        cols = span(t * tile, tile)
        both_g = acc_g[:, cols].reshape(16, 2, 8, tile)
        both_u = acc_u[:, cols].reshape(16, 2, 8, tile)
        pre_gate, tan_gate = both_g[:, 0].reshape(128, tile), both_g[:, 1].reshape(128, tile)
        pre_up, tan_up = both_u[:, 0].reshape(128, tile), both_u[:, 1].reshape(128, tile)
        sig = jax.nn.sigmoid(pre_gate)
        act = pre_gate * sig
        slope = sig * (1.0 + pre_gate * (1.0 - sig))
        coef = pre_up * slope
        th[:, cols] = (slope * tan_gate * pre_up + act * tan_up).astype(BF16)
        acc_g[0:128, cols] = coef
        acc_u[0:128, cols] = act

    loop(0, hidden // tile, finish)
    own = xg[:, span(me * feat, feat)].astype(F32).reshape(16, 2, 8, feat)
    vc[...] = own[:, 1].reshape(128, feat)

    def forward_drain(f):
        for k in (1, 2, 3):
            gather_z(f, k).wait_send()
        for k in range(NZ):
            gather_x(f, k).wait_send()
        gather_c(f).wait_send()

    loop(0, nf, forward_drain)


    def cols_of(xx, cc):
        return span((xx * 2 + cc) * feat, feat)

    def features(k, xx, cc):
        return span(index_of(z + NZ - k, xx, cc) * feat, feat)

    def rs_c(i, xx):
        return remote(
            pbuf.at[i * 2 + xx, :, span((1 - c) * feat, feat)], rb.at[i, :, span(xx * feat, feat)],
            s_send.at[i, xx], s_recv.at[i, xx], c_peer,
        )

    def rs_x(i):
        return remote(xsb.at[i], xrb.at[i], s_send.at[i, 2], s_recv.at[i, 2], x_peer)

    def rs_z(i):
        return remote(
            zsb.at[i], zrb.at[i], s_send.at[i, 3], s_recv.at[i, 3], index_of(z + 1 + i, x, c)
        )

    def summed_c(i, xx):
        return pbuf[i * 2 + xx, :, span(c * feat, feat)] + rb[i, :, span(xx * feat, feat)]

    def middle_step(s):
        @pl.when(s < NZ)
        def _():
            down(s).wait()

            def tile(t):
                cols = span(t * feat, feat)
                held = nn(th[...], dn[s, :, cols])
                pbuf[s * 2 + t // 2, :, span((t % 2) * feat, feat)] = held

            loop(0, 4, tile)
            rs_c(s, 0).start()
            rs_c(s, 1).start()

        @pl.when((s >= 1) & (s <= NZ))
        def _():
            i = s - 1
            rs_c(i, 0).wait_recv()
            rs_c(i, 1).wait_recv()
            xsb[i] = (summed_c(i, 1 - x)).astype(BF16)
            rs_x(i).start()

        @pl.when((s >= 2) & (s <= NZ))
        def _():
            i = s - 2
            rs_x(i).wait_recv()
            total = summed_c(i, x) + xrb[i].astype(F32)
            zsb[i] = total.astype(BF16)
            rs_z(i).start()

    loop(0, NZ + 1, middle_step)
    last = NZ - 1
    rs_x(last).wait_recv()
    total = summed_c(last, x) + xrb[last].astype(F32) + vc[...]
    for i in range(NZ - 1):
        rs_z(i).wait_recv()
        total = total + zrb[i].astype(F32)

    high = total.astype(BF16)
    low = (total - high.astype(F32)).astype(BF16)
    part = nn(high, sk_ref[...]) + nn(low, sk_ref[...])
    sk[...] = part.T.reshape(sk.shape)
    copy_c = remote(sk.at[:, :, 1 - c], rc, k_send.at[0], k_recv.at[0], c_peer)
    copy_c.start()
    copy_c.wait_recv()
    sxs[...] = sk[:, 1 - x, c] + rc[:, 1 - x]
    copy_x = remote(sxs, sxr, k_send.at[1], k_recv.at[1], x_peer)
    copy_x.start()
    copy_x.wait_recv()
    szs[...] = sk[:, x, c] + rc[:, x] + sxr[...]
    copies = [
        remote(szs.at[(z + k) % NZ], szr.at[k - 1], k_send.at[1 + k], k_recv.at[1 + k],
               index_of(z + k, x, c))
        for k in (1, 2, 3)
    ]
    for copy in copies:
        copy.start()
    value = szs[z]
    for k, copy in enumerate(copies):
        copy.wait_recv()
        value = value + szr[k]
    for copy in copies + [copy_c, copy_x]:
        copy.wait_send()

    wga[z, x, c] = (prec_ref[...] * value).astype(BF16)
    mine = wga.at[z, x, c]
    copies = [
        remote(mine, mine, w_send.at[k - 1], w_recv.at[k - 1], index_of(z + k, x, c))
        for k in (1, 2, 3)
    ]
    for copy in copies:
        copy.start()
    for copy in copies:
        copy.wait_recv()
    copy_x = remote(wga.at[:, x, c], wga.at[:, x, c], w_send.at[3], w_recv.at[3], x_peer)
    copy_x.start()
    copy_x.wait_recv()
    copy_c = remote(wga.at[:, :, c], wga.at[:, :, c], w_send.at[4], w_recv.at[4], c_peer)
    copy_c.start()
    copy_c.wait_recv()
    for copy in copies + [copy_x, copy_c]:
        copy.wait_send()
    flat = wga[...].reshape(-1, 128).astype(F32).T.astype(BF16)
    cot = nt(flat, sk_ref[...])
    cot_own[...] = cot

    xg[0:128, features(0, x, c)] = cot.astype(BF16)

    half = 64

    def ag_z(h, k):
        part = xg.at[pl.ds(h * half, half), features(0, x, c)]
        return remote(part, part, a_send.at[h, k], a_recv.at[h, k], index_of(z + k, x, c))

    def ag_x(h, k):
        part = xg.at[pl.ds(h * half, half), features(k, x, c)]
        return remote(part, part, a_send.at[2 + h, k], a_recv.at[2 + h, k], x_peer)

    def ag_c(k, own):
        part = xg.at[pl.ds(0, 128), features(k, x if own else 1 - x, c)]
        row = 4 if own else 5
        return remote(part, part, a_send.at[row, k], a_recv.at[row, k], c_peer)

    def use(k, xx, cc):
        acc_g[128:256, :] += nt(xg[0:128, features(k, xx, cc)], dn[3 - k, :, cols_of(xx, cc)])

    for h in (0, 1):
        for k in (1, 2, 3):
            ag_z(h, k).start()
        ag_x(h, 0).start()
    ag_c(0, True).start()
    acc_g[128:256, :] = jnp.zeros((128, acc_g.shape[1]), F32)
    use(0, x, c)
    for h in (0, 1):
        for k in (1, 2, 3):
            ag_z(h, k).wait_recv()
            ag_x(h, k).start()
            if h:
                ag_c(k, True).start()

    def own_column(k):
        use(k, x, c)

    loop(1, NZ, own_column)

    def pass_on(k):
        ag_x(0, k).wait_recv()
        ag_x(1, k).wait_recv()
        ag_c(k, False).start()

    loop(0, NZ, pass_on)

    def sibling_own(k):
        ag_c(k, True).wait_recv()
        use(k, x, 1 - c)

    loop(0, NZ, sibling_own)

    def other_column(k):
        use(k, 1 - x, c)

    loop(0, NZ, other_column)

    def sibling_other(k):
        ag_c(k, False).wait_recv()
        use(k, 1 - x, 1 - c)

    loop(0, NZ, sibling_other)

    th[...] = (acc_g[128:256, :] * acc_g[0:128, :]).astype(BF16)
    bu[...] = (acc_g[128:256, :] * acc_u[0:128, :]).astype(BF16)

    def middle_drain(k):
        @pl.when(k >= 1)
        def _():
            ag_z(0, k).wait_send()
            ag_z(1, k).wait_send()
            rs_z(k - 1).wait_send()

        ag_x(0, k).wait_send()
        ag_x(1, k).wait_send()
        ag_c(k, True).wait_send()
        ag_c(k, False).wait_send()
        rs_c(k, 0).wait_send()
        rs_c(k, 1).wait_send()
        rs_x(k).wait_send()

    loop(0, NZ, middle_drain)

    half_c = fc // 2

    def back_c(f):
        return remote(
            pbuf.at[f, span((1 - c) * 64, 64)], rb.at[f // 2, span((f % 2) * 64, 64)], c_send.at[f], c_recv.at[f], c_peer
        )

    def back_x(f):
        return remote(bxs.at[f], bxr.at[f], x_send.at[f], x_recv.at[f], x_peer)

    def back_z(f, k):
        return remote(
            bzs.at[f, k - 1], bzr.at[f, k - 1], z_send.at[f, k - 1], z_recv.at[f, k - 1],
            index_of(z + k, x, c),
        )

    def final_step(s):
        @pl.when(s < nf)
        def _():

            def piece(h):
                g = (nf + s) * parts + h
                arrive(g)
                slot = lax.rem(g, slots)
                pbuf[s, :, span(h * wc, wc)] = nt(th[...], wg[slot]) + nt(bu[...], wu[slot])

                @pl.when(g + slots < 2 * nf * parts)
                def _():
                    fetch(g + slots)

            loop(0, parts, piece)

            @pl.when(s == (me * feat) // fc)
            def _():
                cols = span(((me * feat) % fc) // feat * feat, feat)
                pbuf[s, :, cols] += cot_own[...]

            back_c(s).start()

        @pl.when((s >= 1) & (s <= nf))
        def _():
            f = s - 1
            back_c(f).wait_recv()
            away = pbuf[f, span(c * 64 + (1 - x) * 32, 32)] + rb[f // 2, span((f % 2) * 64 + (1 - x) * 32, 32)]
            bxs[f] = away.astype(BF16)
            back_x(f).start()

        @pl.when((s >= 2) & (s <= nf + 1))
        def _():
            f = s - 2
            back_x(f).wait_recv()
            tb[...] = (
                pbuf[f, span(c * 64 + x * 32, 32)]
                + rb[f // 2, span((f % 2) * 64 + x * 32, 32)]
                + bxr[f].astype(F32)
            )
            for k in (1, 2, 3):
                rows = tb[span(((z + k) % NZ) * 8, 8), :]
                folded = jnp.concatenate([rows[:, :half_c], rows[:, half_c:]], axis=0)
                bzs[f, k - 1] = folded.astype(BF16)
                back_z(f, k).start()
            out_ref[:, span(f * fc, fc)] = tb[span(z * 8, 8), :]

        @pl.when(s >= 3)
        def _():
            f = s - 3
            total = out_ref[:, span(f * fc, fc)]
            for k in (1, 2, 3):
                back_z(f, k).wait_recv()
                folded = bzr[f, k - 1].astype(F32)
                total = total + jnp.concatenate([folded[:8], folded[8:]], axis=1)
            out_ref[:, span(f * fc, fc)] = total

    loop(0, nf + 3, final_step)

    def final_drain(f):
        back_c(f).wait_send()
        back_x(f).wait_send()
        for k in (1, 2, 3):
            back_z(f, k).wait_send()

    loop(0, nf, final_drain)


def rows_kernel(ids_ref, table_ref, out_ref, buf, sem):
    count = out_ref.shape[1]
    unroll = 8

    def token(t):
        block = ((t // 8) % NZ) * 4 + ((t // 32) % NX) * 2 + t // 64
        return ids_ref[block * 8 + t % 8]

    def copy(t):
        block = pl.multiple_of(lax.shift_right_logical(token(t), 7) * 128, 128)
        return pltpu.make_async_copy(table_ref.at[:, pl.ds(block, 128)], buf.at[t], sem.at[t])

    def start(g):
        for r in range(unroll):
            copy(g * unroll + r).start()

    loop(0, count // unroll, start)
    lanes = lax.broadcasted_iota(jnp.int32, out_ref.shape, 1)

    def step(g, held):
        first = g * unroll
        for r in range(unroll):
            copy(first + r).wait()
        for r in range(unroll):
            t = first + r
            block = buf[t].astype(F32)
            shift = jnp.bitwise_and(t + 128 - jnp.bitwise_and(token(t), 127), 127)
            held = jnp.where(lanes == t, pltpu.roll(block, shift, axis=1), held)
        return held

    out_ref[...] = lax.fori_loop(0, count // unroll, step, jnp.zeros(out_ref.shape, F32))


ANY = pl.BlockSpec(memory_space=pl.ANY)
IN_VMEM = pl.BlockSpec(memory_space=pltpu.VMEM)


def params(collective_id):
    return pltpu.CompilerParams(
        collective_id=collective_id, has_side_effects=True, vmem_limit_bytes=LIMIT
    )


def cost(flops, nbytes):
    return pl.CostEstimate(flops=flops, bytes_accessed=nbytes, transcendentals=0)


def fast(inputs, tangent, token_ids, gate_weight, up_weight, down_weight, sketch, teacher_precision):
    model, hidden = gate_weight.shape
    feat, rank = sketch.shape
    coords = teacher_precision.shape[1]
    rows = token_ids.shape[0]
    fc = 1024
    nf = model // fc
    shape = jax.ShapeDtypeStruct

    prec = pl.pallas_call(
        rows_kernel,
        out_shape=shape((coords, rows), F32),
        in_specs=[pl.BlockSpec(memory_space=pltpu.SMEM), ANY],
        out_specs=IN_VMEM,
        scratch_shapes=[VMEM((rows, coords, 128), BF16), DMA((rows,))],
        name="precision_rows",
    )(token_ids, teacher_precision.T)

    slots = 2
    wc = fc // 2
    width = model // NZ
    return pl.pallas_call(
        functools.partial(kernel, nf, fc, wc, slots, min(3, nf), feat),
        out_shape=shape((8, model), F32),
        in_specs=[IN_VMEM] * 4 + [ANY] * 3,
        out_specs=IN_VMEM,
        scratch_shapes=[
            VMEM((2 * rows, model), BF16),
            VMEM((slots, wc, hidden), BF16),
            VMEM((slots, wc, hidden), BF16),
            VMEM((2 * rows, hidden), F32),
            VMEM((2 * rows, hidden), F32),
            VMEM((rows, hidden), BF16), VMEM((rows, hidden), BF16),
            VMEM((rows, feat), F32), VMEM((rows, feat), F32),
            VMEM((NZ, hidden, width), BF16),
            VMEM((nf, rows, fc), F32),
            VMEM((NZ, rows, 2 * feat), F32),
            VMEM((NZ, rows, feat), BF16), VMEM((NZ, rows, feat), BF16),
            VMEM((3, rows, feat), BF16), VMEM((3, rows, feat), BF16),
            VMEM((NZ, NX, NC, coords, rows), F32),
            VMEM((NZ, NX, coords, rows), F32),
            VMEM((NZ, coords, rows), F32), VMEM((NZ, coords, rows), F32),
            VMEM((NZ, coords, rows), F32), VMEM((3, coords, rows), F32),
            VMEM((NZ, NX, NC, coords, rows), BF16),
            VMEM((nf, 32, fc), BF16), VMEM((nf, 32, fc), BF16),
            VMEM((nf, 3, 16, fc // 2), BF16), VMEM((nf, 3, 16, fc // 2), BF16),
            VMEM((32, fc), F32),
            DMA((2, slots)), DMA((NZ,)),
            DMA((nf, 3)), DMA((nf, 3)),
            DMA((nf, NZ)), DMA((nf, NZ)),
            DMA((nf,)), DMA((nf,)),
            DMA((NZ, 4)), DMA((NZ, 4)),
            DMA((5,)), DMA((5,)),
            DMA((5,)), DMA((5,)),
            DMA((6, NZ)), DMA((6, NZ)),
            DMA((nf,)), DMA((nf,)),
            DMA((nf,)), DMA((nf,)),
            DMA((nf, 3)), DMA((nf, 3)),
        ],
        compiler_params=params(0),
        cost_estimate=cost(16 * rows * model * hidden, 10 * model * hidden),
        name="gauss_newton",
    )(inputs, tangent, sketch, prec, gate_weight, up_weight, down_weight)


def general(inputs, tangent, token_ids, gate_weight, up_weight, down_weight, sketch, teacher_precision):
    rows_x, rows_v = (
        lax.all_gather(inputs, "tensor", axis=0, tiled=True),
        lax.all_gather(tangent, "tensor", axis=0, tiled=True),
    )
    position = lax.axis_index("tensor")
    feat_local = sketch.shape[0]
    offset = position * feat_local
    pre_gate = jnp.dot(rows_x, gate_weight, preferred_element_type=F32)
    pre_up = jnp.dot(rows_x, up_weight, preferred_element_type=F32)
    tan_gate = jnp.dot(rows_v, gate_weight, preferred_element_type=F32)
    tan_up = jnp.dot(rows_v, up_weight, preferred_element_type=F32)
    sig = jax.nn.sigmoid(pre_gate)
    act = pre_gate * sig
    slope = sig * (1.0 + pre_gate * (1.0 - sig))
    tan_hidden = (slope * tan_gate * pre_up + act * tan_up).astype(BF16)
    v_mine = lax.dynamic_slice_in_dim(rows_v, offset, feat_local, 1)
    own_term = jnp.dot(v_mine, sketch, preferred_element_type=F32)
    partial_value = jnp.dot(tan_hidden, down_weight, preferred_element_type=F32)
    summed_cols = lax.psum_scatter(partial_value, "tensor", scatter_dimension=1, tiled=True)
    sketch_part = (
        jnp.dot(summed_cols, sketch.astype(F32), precision=lax.Precision.HIGHEST) + own_term
    )
    sketch_cols = lax.psum_scatter(sketch_part, "tensor", scatter_dimension=1, tiled=True)
    rows_prec = teacher_precision[token_ids].astype(F32)
    weighted_cols = (rows_prec * sketch_cols).astype(BF16)
    weighted = lax.all_gather(weighted_cols, "tensor", axis=1, tiled=True)
    cot_cols = jnp.dot(weighted, sketch.T, preferred_element_type=F32)
    cot_full = lax.all_gather(cot_cols.astype(BF16), "tensor", axis=1, tiled=True)
    back_hidden = jnp.dot(cot_full, down_weight.T, preferred_element_type=F32)
    back_gate = (back_hidden * pre_up * slope).astype(BF16)
    back_up = (back_hidden * act).astype(BF16)
    result = jnp.dot(back_gate, gate_weight.T, preferred_element_type=F32)
    result = result + jnp.dot(back_up, up_weight.T, preferred_element_type=F32)
    current = lax.dynamic_slice_in_dim(result, offset, feat_local, 1)
    return lax.psum_scatter(
        lax.dynamic_update_slice_in_dim(result, current + cot_cols, offset, 1),
        "tensor",
        scatter_dimension=0,
        tiled=True,
    )


def solution(mesh):
    on_device = fast if mesh.shape["tensor"] == NZ * NX * NC else general
    return jax.shard_map(
        on_device,
        mesh=mesh,
        in_specs=(
            P(("groups", "tensor"), None),
            P(("groups", "tensor"), None),
            P("groups"),
            P(None, "tensor"),
            P(None, "tensor"),
            P("tensor", None),
            P("tensor", None),
            P(None, "tensor"),
        ),
        out_specs=P(("groups", "tensor"), None),
        check_vma=False,
    )
```

time: 180 us -> 162 us (0.900)
  Pallas kernels: 175 us -> 160 us
    pallas_call x4 -> x2, Pallas kernels: 175 us -> 160 us  [the longest x1 151 us: fast(): pl.pallas_call(functools.partial(kernel, nf, fc, wc, slots, min(3, nf), f...]
where the time goes in v2:
time: 162 us; the launch traced here: 161 us
  Pallas kernels  160 us (99%)
  local copies, waits for them, and re-layouts  1.67 us (1%)
    pallas_call x1, Pallas kernels, fast(): pl.pallas_call(functools.partial(kernel, nf, fc, wc, slots, min(3, nf), f...  151 us
    pallas_call x1, Pallas kernels, fast(): pl.pallas_call(rows_kernel, out_shape=shape((coords, rows), F32), in_spec...  9.1 us

profile of v2, /device:TPU:0, one launch (start us, length us, event | category | flops | bytes accessed | tf_op | source)
XLA Modules:
  0.0 161.3 jit_solution(1791885121670035731)
XLA Ops:
  0.0 9.1 %precision_rows.1.prec_ref = f32[64,128]{1,0:T(8,128)} custom-call(s32[128]{0:T(128)} %ids_ref.1, bf16[64,64128]{1,0:T(8,128)(2,1)} %bitcast.1), custom_call_target="tpu_custom_call" | custom-call | tf_op jit(solution)/shard_map/precision_rows/pallas_call | solution.py:541
  9.1 150.6 %gauss_newton.1 = f32[8,8192]{1,0:T(8,128)} custom-call(bf16[8,8192]{1,0:T(8,128)(2,1)} %in_ref.1, bf16[8,8192]{1,0:T(8,128)(2,1)} %tan_ref.1, bf16[512,1024]{1,0:T(8,128)(2,1)} %sk_ref.1, f32[64,128]{1,0:T(8,128)} %precision_rows.1.prec_ref, bf16[8192,1792]{1,0:T(8,128)(2,1)} %gate_ref.1, bf16[8192,1792]{1,0:T(8,128)(2,1)} %up_ref.1, ...), custom_call_target="tpu_custom_call" | custom-call | flops 30064771072 | bytes 146800640 | tf_op jit(solution)/shard_map/gauss_newton/pallas_call | solution.py:553
  159.7 1.7 %copy.10 = f32[8,8192]{1,0:T(8,128)} copy(f32[8,8192]{1,0:T(8,128)} %gauss_newton.1) | data formatting | bytes 524288
